TPU v7x, 512 devices: a whole 4x8x8 slice. The times are simulated.
512 devices in a mesh: energy: 16 (over x, y_hi), width: 32 (over z, y_lo, core).
Axes of the slice: x: 4, y: 8 (y_hi: 4, y_lo: 2; y = y_hi * 2 + y_lo), z: 8, core: 2. Of those that a mesh axis runs over, the one named last changes fastest.
Arguments:
- inverse_blocks: bfloat16 [32, 8192, 256], P('energy', 'width')
- source: bfloat16 [32, 8192, 512], P('energy', 'width'), may hold values from -6 to 6
- left_coupling: bfloat16 [1024, 256], P('width'), may hold values from -0.875 to 0.875
- right_coupling: bfloat16 [1024, 256], P('width'), may hold values from -0.875 to 0.875
- energy_weights: float32 [32], P('energy'), may hold values from 0.25 to 2
- collector_low: int32 [32], P('width'), may hold values from 0 to 63
- collector_high: int32 [32], P('width'), may hold values from 193 to 256
Outputs:
- gradient: float32 [32, 256, 256], P('width', 'energy')
Inputs may be any that keep to these rules, and one draw needn't show every extreme that they name: collector_low < 64 and collector_high > 192 for every strip.
All inputs are finite; a program needn't handle non-finite values.
Results may differ from a plain program's by a relative error of at most 0.0033.
Values may be sent and summed in bfloat16 or wider, within the bound.
No kernel may reach another device: no remote copies, remote signals or barrier semaphores. Data moves between devices by JAX's collectives and lax.ppermute only.
A program may use at most 64 MiB of HBM per device.

v0:
```python
import jax
import jax.numpy as jnp
from jax import lax
from jax.sharding import PartitionSpec as P

SWEEPS = 10


def with_halo(block, sides, width):
    for axis, dim in sides:
        count = lax.axis_size(axis)
        forward = [(i, i + 1) for i in range(count - 1)]
        forward.append((count - 1, 0))
        backward = [(target, source) for source, target in forward]
        low = lax.ppermute(
            lax.slice_in_dim(block, block.shape[dim] - width, None, axis=dim), axis, forward
        )
        high = lax.ppermute(lax.slice_in_dim(block, 0, width, axis=dim), axis, backward)
        block = jnp.concatenate([low, block, high], axis=dim)
    return block


def couple_rows(left_coupling, right_coupling, tails, heads):
    first = jnp.einsum("ei,kem->kim", left_coupling, tails, preferred_element_type=jnp.float32)
    second = jnp.einsum("ei,kem->kim", right_coupling, heads, preferred_element_type=jnp.float32)
    return first + second


def body(
    inverse_blocks,
    source,
    left_coupling,
    right_coupling,
    energy_weights,
    collector_low,
    collector_high,
):
    edge = left_coupling.shape[0]
    block = inverse_blocks.shape[1]
    count = inverse_blocks.shape[0]
    modes = source.shape[2]
    psi = jnp.einsum(
        "kij,kjm->kim", inverse_blocks, source, preferred_element_type=jnp.float32
    ).astype(jnp.bfloat16)

    def forward_sweep(sweep, psi):
        padded = with_halo(psi, (("width", 1),), edge)
        tails = padded[:, :edge]
        heads = padded[:, padded.shape[1] - edge :]
        couple = couple_rows(left_coupling, right_coupling, tails, heads)
        rhs = (source.astype(jnp.float32) + couple).astype(jnp.bfloat16)
        return jnp.einsum(
            "kij,kjm->kim", inverse_blocks, rhs, preferred_element_type=jnp.float32
        ).astype(jnp.bfloat16)

    psi = lax.fori_loop(0, SWEEPS - 1, forward_sweep, psi)
    rows = lax.iota(jnp.int32, block)
    mask = ((rows >= collector_low[0]) & (rows < collector_high[0])).astype(jnp.float32)
    adjoint_source = (
        2.0 * energy_weights[:, None, None] * mask[None, :, None] * psi.astype(jnp.float32)
    )
    lam = jnp.einsum(
        "kji,kjm->kim",
        inverse_blocks,
        adjoint_source.astype(jnp.bfloat16),
        preferred_element_type=jnp.float32,
    ).astype(jnp.bfloat16)
    middle = jnp.zeros((count, block - 2 * edge, modes), jnp.float32)

    def adjoint_sweep(sweep, lam):
        to_prev = jnp.einsum(
            "ei,kim->kem", left_coupling, lam, preferred_element_type=jnp.float32
        ).astype(jnp.bfloat16)
        to_next = jnp.einsum(
            "ei,kim->kem", right_coupling, lam, preferred_element_type=jnp.float32
        ).astype(jnp.bfloat16)
        outgoing = jnp.concatenate([to_prev, to_next], axis=1)
        padded = with_halo(outgoing, (("width", 1),), edge)
        from_prev = padded[:, :edge]
        from_next = padded[:, padded.shape[1] - edge :]
        extra = jnp.concatenate(
            [from_prev.astype(jnp.float32), middle, from_next.astype(jnp.float32)], axis=1
        )
        update = (adjoint_source + extra).astype(jnp.bfloat16)
        return jnp.einsum(
            "kji,kjm->kim", inverse_blocks, update, preferred_element_type=jnp.float32
        ).astype(jnp.bfloat16)

    lam = lax.fori_loop(0, SWEEPS - 1, adjoint_sweep, lam)
    owned = block // lax.axis_size("energy")
    product = jnp.einsum("kim,kjm->ij", lam, psi, preferred_element_type=jnp.float32)
    full = lax.psum(product * (-1.0 / modes), "energy")
    mine = lax.dynamic_slice_in_dim(full, lax.axis_index("energy") * owned, owned, 0)
    return mine.reshape(1, owned, block)


def solution(mesh):
    placed = (
        P("energy", "width", None),
        P("energy", "width", None),
        P("width", None),
        P("width", None),
        P("energy"),
        P("width"),
        P("width"),
    )
    return jax.shard_map(
        body, mesh=mesh, in_specs=placed, out_specs=P("width", "energy", None), check_vma=False
    )
```

profile of v0, /device:TPU:64, one launch (start us, length us, event | category | flops | bytes accessed | tf_op | source)
XLA Modules:
  0.0 456.8 jit_solution(2762212867480273165)
XLA Ops:
  9.8 123.9 %while.20 = (s32[]{:T(128)}, bf16[2,256,512]{1,2,0:T(8,128)(2,1)S(1)}, bf16[2,256,512]{1,2,0:T(8,128)(2,1)S(1)}, bf16[32,256]{1,0:T(8,128)(2,1)S(1)}, bf16[32,25...) while((s32[]{:T(128)}, bf16[2,256,512]{1,2,0:T(8,128)(2,1)S(1)}, ...), condition=%wide.region_1.0_spmd, body=%wide.region_0.0_spmd.sunk | while | flops 169082880 | bytes 4358301 | solution.py:56
  10.0 2.0 collective-permute-start
  12.0 2.3 collective-permute-start.1
  16.2 4.5 collective-permute-done.1
  21.3 1.9 collective-permute-start
  23.2 2.4 collective-permute-start.1
  25.6 2.3 collective-permute-done
  28.2 7.1 %collective-permute-done.1 = bf16[2,32,512]{1,2,0:T(8,128)(2,1)S(1)} collective-permute-done((bf16[2,32,512]{1,2,0:T(8,128)(2,1)S(1)}, bf16[2,32,512]{1,2,0:T(8,128)(2,1)S(1)}, u32[]{:S(2)}, u32[]{:S(2)}) %collective-permute-start.1) | collective-permute-done | bytes 65568 | tf_op jit(solution)/shard_map/while/body/eval_jaxpr/ppermute | solution.py:15
  36.0 1.9 collective-permute-start
  37.9 2.4 collective-permute-start.1
  40.3 2.5 collective-permute-done
  43.1 8.8 %collective-permute-done.1 = bf16[2,32,512]{1,2,0:T(8,128)(2,1)S(1)} collective-permute-done((bf16[2,32,512]{1,2,0:T(8,128)(2,1)S(1)}, bf16[2,32,512]{1,2,0:T(8,128)(2,1)S(1)}, u32[]{:S(2)}, u32[]{:S(2)}) %collective-permute-start.1) | collective-permute-done | bytes 65568 | tf_op jit(solution)/shard_map/while/body/eval_jaxpr/ppermute | solution.py:15
  52.5 1.9 collective-permute-start
  54.4 2.4 collective-permute-start.1
  56.9 2.5 collective-permute-done
  59.6 4.7 %collective-permute-done.1 = bf16[2,32,512]{1,2,0:T(8,128)(2,1)S(1)} collective-permute-done((bf16[2,32,512]{1,2,0:T(8,128)(2,1)S(1)}, bf16[2,32,512]{1,2,0:T(8,128)(2,1)S(1)}, u32[]{:S(2)}, u32[]{:S(2)}) %collective-permute-start.1) | collective-permute-done | bytes 65568 | tf_op jit(solution)/shard_map/while/body/eval_jaxpr/ppermute | solution.py:15
  64.9 1.9 collective-permute-start
  66.9 2.4 collective-permute-start.1
  69.3 2.5 collective-permute-done
  72.0 4.7 %collective-permute-done.1 = bf16[2,32,512]{1,2,0:T(8,128)(2,1)S(1)} collective-permute-done((bf16[2,32,512]{1,2,0:T(8,128)(2,1)S(1)}, bf16[2,32,512]{1,2,0:T(8,128)(2,1)S(1)}, u32[]{:S(2)}, u32[]{:S(2)}) %collective-permute-start.1) | collective-permute-done | bytes 65568 | tf_op jit(solution)/shard_map/while/body/eval_jaxpr/ppermute | solution.py:15
  77.4 1.9 collective-permute-start
  79.3 2.4 collective-permute-start.1
  81.7 2.5 collective-permute-done
  84.4 4.7 %collective-permute-done.1 = bf16[2,32,512]{1,2,0:T(8,128)(2,1)S(1)} collective-permute-done((bf16[2,32,512]{1,2,0:T(8,128)(2,1)S(1)}, bf16[2,32,512]{1,2,0:T(8,128)(2,1)S(1)}, u32[]{:S(2)}, u32[]{:S(2)}) %collective-permute-start.1) | collective-permute-done | bytes 65568 | tf_op jit(solution)/shard_map/while/body/eval_jaxpr/ppermute | solution.py:15
  89.9 1.9 collective-permute-start
  91.8 2.4 collective-permute-start.1
  94.2 2.5 collective-permute-done
  96.9 6.0 %collective-permute-done.1 = bf16[2,32,512]{1,2,0:T(8,128)(2,1)S(1)} collective-permute-done((bf16[2,32,512]{1,2,0:T(8,128)(2,1)S(1)}, bf16[2,32,512]{1,2,0:T(8,128)(2,1)S(1)}, u32[]{:S(2)}, u32[]{:S(2)}) %collective-permute-start.1) | collective-permute-done | bytes 65568 | tf_op jit(solution)/shard_map/while/body/eval_jaxpr/ppermute | solution.py:15
  103.7 1.9 collective-permute-start
  105.6 2.4 collective-permute-start.1
  108.0 2.5 collective-permute-done
  110.7 7.3 %collective-permute-done.1 = bf16[2,32,512]{1,2,0:T(8,128)(2,1)S(1)} collective-permute-done((bf16[2,32,512]{1,2,0:T(8,128)(2,1)S(1)}, bf16[2,32,512]{1,2,0:T(8,128)(2,1)S(1)}, u32[]{:S(2)}, u32[]{:S(2)}) %collective-permute-start.1) | collective-permute-done | bytes 65568 | tf_op jit(solution)/shard_map/while/body/eval_jaxpr/ppermute | solution.py:15
  118.8 1.9 collective-permute-start
  120.7 2.4 collective-permute-start.1
  123.1 2.5 collective-permute-done
  125.8 7.4 %collective-permute-done.1 = bf16[2,32,512]{1,2,0:T(8,128)(2,1)S(1)} collective-permute-done((bf16[2,32,512]{1,2,0:T(8,128)(2,1)S(1)}, bf16[2,32,512]{1,2,0:T(8,128)(2,1)S(1)}, u32[]{:S(2)}, u32[]{:S(2)}) %collective-permute-start.1) | collective-permute-done | bytes 65568 | tf_op jit(solution)/shard_map/while/body/eval_jaxpr/ppermute | solution.py:15
  134.1 137.8 %while.21 = (s32[]{:T(128)}, bf16[2,256,512]{1,2,0:T(8,128)(2,1)S(1)}, bf16[32,256]{1,0:T(8,128)(2,1)S(1)}, bf16[32,256]{1,0:T(8,128)(2,1)S(1)}, f32[2,256,512]{...) while((s32[]{:T(128)}, bf16[2,256,512]{1,2,0:T(8,128)(2,1)S(1)}, ...), condition=%wide.region_3.0_spmd, body=%wide.region_2.0_spmd.sunk | while | flops 169213952 | bytes 4230837 | solution.py:89
  134.4 1.9 collective-permute-start.2
  136.6 2.4 collective-permute-start.3
  141.0 7.9 %collective-permute-done.3 = bf16[2,32,512]{1,2,0:T(8,128)(2,1)S(1)} collective-permute-done((bf16[2,32,512]{1,2,0:T(8,128)(2,1)S(1)}, bf16[2,32,512]{1,2,0:T(8,128)(2,1)S(1)}, u32[]{:S(2)}, u32[]{:S(2)}) %collective-permute-start.3) | collective-permute-done | bytes 65568 | tf_op jit(solution)/shard_map/while/body/eval_jaxpr/ppermute | solution.py:15
  149.6 1.9 collective-permute-start.2
  151.8 2.4 collective-permute-start.3
  156.1 7.6 %collective-permute-done.3 = bf16[2,32,512]{1,2,0:T(8,128)(2,1)S(1)} collective-permute-done((bf16[2,32,512]{1,2,0:T(8,128)(2,1)S(1)}, bf16[2,32,512]{1,2,0:T(8,128)(2,1)S(1)}, u32[]{:S(2)}, u32[]{:S(2)}) %collective-permute-start.3) | collective-permute-done | bytes 65568 | tf_op jit(solution)/shard_map/while/body/eval_jaxpr/ppermute | solution.py:15
  164.4 1.9 collective-permute-start.2
  166.6 2.4 collective-permute-start.3
  171.0 8.1 %collective-permute-done.3 = bf16[2,32,512]{1,2,0:T(8,128)(2,1)S(1)} collective-permute-done((bf16[2,32,512]{1,2,0:T(8,128)(2,1)S(1)}, bf16[2,32,512]{1,2,0:T(8,128)(2,1)S(1)}, u32[]{:S(2)}, u32[]{:S(2)}) %collective-permute-start.3) | collective-permute-done | bytes 65568 | tf_op jit(solution)/shard_map/while/body/eval_jaxpr/ppermute | solution.py:15
  179.8 1.9 collective-permute-start.2
  182.0 2.4 collective-permute-start.3
  186.3 8.1 %collective-permute-done.3 = bf16[2,32,512]{1,2,0:T(8,128)(2,1)S(1)} collective-permute-done((bf16[2,32,512]{1,2,0:T(8,128)(2,1)S(1)}, bf16[2,32,512]{1,2,0:T(8,128)(2,1)S(1)}, u32[]{:S(2)}, u32[]{:S(2)}) %collective-permute-start.3) | collective-permute-done | bytes 65568 | tf_op jit(solution)/shard_map/while/body/eval_jaxpr/ppermute | solution.py:15
  195.1 1.9 collective-permute-start.2
  197.3 2.4 collective-permute-start.3
  201.7 8.2 %collective-permute-done.3 = bf16[2,32,512]{1,2,0:T(8,128)(2,1)S(1)} collective-permute-done((bf16[2,32,512]{1,2,0:T(8,128)(2,1)S(1)}, bf16[2,32,512]{1,2,0:T(8,128)(2,1)S(1)}, u32[]{:S(2)}, u32[]{:S(2)}) %collective-permute-start.3) | collective-permute-done | bytes 65568 | tf_op jit(solution)/shard_map/while/body/eval_jaxpr/ppermute | solution.py:15
  210.6 1.9 collective-permute-start.2
  212.8 2.4 collective-permute-start.3
  217.1 8.2 %collective-permute-done.3 = bf16[2,32,512]{1,2,0:T(8,128)(2,1)S(1)} collective-permute-done((bf16[2,32,512]{1,2,0:T(8,128)(2,1)S(1)}, bf16[2,32,512]{1,2,0:T(8,128)(2,1)S(1)}, u32[]{:S(2)}, u32[]{:S(2)}) %collective-permute-start.3) | collective-permute-done | bytes 65568 | tf_op jit(solution)/shard_map/while/body/eval_jaxpr/ppermute | solution.py:15
  226.0 1.9 collective-permute-start.2
  228.2 2.4 collective-permute-start.3
  232.5 8.2 %collective-permute-done.3 = bf16[2,32,512]{1,2,0:T(8,128)(2,1)S(1)} collective-permute-done((bf16[2,32,512]{1,2,0:T(8,128)(2,1)S(1)}, bf16[2,32,512]{1,2,0:T(8,128)(2,1)S(1)}, u32[]{:S(2)}, u32[]{:S(2)}) %collective-permute-start.3) | collective-permute-done | bytes 65568 | tf_op jit(solution)/shard_map/while/body/eval_jaxpr/ppermute | solution.py:15
  241.4 1.9 collective-permute-start.2
  243.6 2.4 collective-permute-start.3
  248.0 8.2 %collective-permute-done.3 = bf16[2,32,512]{1,2,0:T(8,128)(2,1)S(1)} collective-permute-done((bf16[2,32,512]{1,2,0:T(8,128)(2,1)S(1)}, bf16[2,32,512]{1,2,0:T(8,128)(2,1)S(1)}, u32[]{:S(2)}, u32[]{:S(2)}) %collective-permute-start.3) | collective-permute-done | bytes 65568 | tf_op jit(solution)/shard_map/while/body/eval_jaxpr/ppermute | solution.py:15
  259.0 2.4 collective-permute-start.3
  263.4 8.2 %collective-permute-done.3 = bf16[2,32,512]{1,2,0:T(8,128)(2,1)S(1)} collective-permute-done((bf16[2,32,512]{1,2,0:T(8,128)(2,1)S(1)}, bf16[2,32,512]{1,2,0:T(8,128)(2,1)S(1)}, u32[]{:S(2)}, u32[]{:S(2)}) %collective-permute-start.3) | collective-permute-done | bytes 65568 | tf_op jit(solution)/shard_map/while/body/eval_jaxpr/ppermute | solution.py:15
  273.0 175.6 %all-reduce.2.cloned.1.call-done = f32[256,256]{1,0:T(8,128)} async-done(((f32[256,256]{1,0:T(8,128)}), f32[256,256]{1,0:T(8,128)}) %all-reduce.2.cloned.1.call-update) | async-done | bytes 262160 | tf_op jit(solution)/shard_map/psum | solution.py:92
  (123 shorter events, 42.2 us)
Async XLA Ops:
  6.5 1.3 copy-start.1
  6.5 1.3 copy-start
  6.5 442.1 %all-reduce.2.cloned.1.call-start = ((), (), s32[]{:S(2)}) async-start(), calls=%async_computation | async-start | bytes 524288 | tf_op jit(solution)/shard_map/psum | solution.py:92
  8.2 1.6 copy-start.4
  8.2 1.6 copy-start.3
  8.4 1.4 copy-start.2
  10.0 5.9 %collective-permute-start = (bf16[2,32,512]{1,2,0:T(8,128)(2,1)S(1)}, bf16[2,32,512]{1,2,0:T(8,128)(2,1)S(1)}, u32[]{:S(2)}, u32[]{:S(2)}) collective-permute-start(bf16[2,32,512]{1,2,0:T(8,128)(2,1)S(1)} %get-tuple-element.173), channel_id=1, source_target_pairs={{1,0},{2,1},{3,2},{4,3},{5,4},{6,5},{7,6},{8,7},{9,8},{10,9},{11,1... | collective-permute-start | bytes 196616 | tf_op jit(solution)/shard_map/while/body/eval_jaxpr/ppermute | solution.py:18
  12.0 8.6 %collective-permute-start.1 = (bf16[2,32,512]{1,2,0:T(8,128)(2,1)S(1)}, bf16[2,32,512]{1,2,0:T(8,128)(2,1)S(1)}, u32[]{:S(2)}, u32[]{:S(2)}) collective-permute-start(bf16[2,32,512]{1,2,0:T(8,128)(2,1)S(1)} %get-tuple-element.174), channel_id=1, source_target_pairs={{0,1},{1,2},{2,3},{3,4},{4,5},{5,6},{6,7},{7,8},{8,9},{9,10},{10,1... | collective-permute-start | bytes 196616 | tf_op jit(solution)/shard_map/while/body/eval_jaxpr/ppermute | solution.py:15
  21.3 6.6 %collective-permute-start = (bf16[2,32,512]{1,2,0:T(8,128)(2,1)S(1)}, bf16[2,32,512]{1,2,0:T(8,128)(2,1)S(1)}, u32[]{:S(2)}, u32[]{:S(2)}) collective-permute-start(bf16[2,32,512]{1,2,0:T(8,128)(2,1)S(1)} %get-tuple-element.173), channel_id=1, source_target_pairs={{1,0},{2,1},{3,2},{4,3},{5,4},{6,5},{7,6},{8,7},{9,8},{10,9},{11,1... | collective-permute-start | bytes 196616 | tf_op jit(solution)/shard_map/while/body/eval_jaxpr/ppermute | solution.py:18
  23.2 12.1 %collective-permute-start.1 = (bf16[2,32,512]{1,2,0:T(8,128)(2,1)S(1)}, bf16[2,32,512]{1,2,0:T(8,128)(2,1)S(1)}, u32[]{:S(2)}, u32[]{:S(2)}) collective-permute-start(bf16[2,32,512]{1,2,0:T(8,128)(2,1)S(1)} %get-tuple-element.174), channel_id=1, source_target_pairs={{0,1},{1,2},{2,3},{3,4},{4,5},{5,6},{6,7},{7,8},{8,9},{9,10},{10,1... | collective-permute-start | bytes 196616 | tf_op jit(solution)/shard_map/while/body/eval_jaxpr/ppermute | solution.py:15
  36.0 6.8 %collective-permute-start = (bf16[2,32,512]{1,2,0:T(8,128)(2,1)S(1)}, bf16[2,32,512]{1,2,0:T(8,128)(2,1)S(1)}, u32[]{:S(2)}, u32[]{:S(2)}) collective-permute-start(bf16[2,32,512]{1,2,0:T(8,128)(2,1)S(1)} %get-tuple-element.173), channel_id=1, source_target_pairs={{1,0},{2,1},{3,2},{4,3},{5,4},{6,5},{7,6},{8,7},{9,8},{10,9},{11,1... | collective-permute-start | bytes 196616 | tf_op jit(solution)/shard_map/while/body/eval_jaxpr/ppermute | solution.py:18
  37.9 13.9 %collective-permute-start.1 = (bf16[2,32,512]{1,2,0:T(8,128)(2,1)S(1)}, bf16[2,32,512]{1,2,0:T(8,128)(2,1)S(1)}, u32[]{:S(2)}, u32[]{:S(2)}) collective-permute-start(bf16[2,32,512]{1,2,0:T(8,128)(2,1)S(1)} %get-tuple-element.174), channel_id=1, source_target_pairs={{0,1},{1,2},{2,3},{3,4},{4,5},{5,6},{6,7},{7,8},{8,9},{9,10},{10,1... | collective-permute-start | bytes 196616 | tf_op jit(solution)/shard_map/while/body/eval_jaxpr/ppermute | solution.py:15
  52.5 6.8 %collective-permute-start = (bf16[2,32,512]{1,2,0:T(8,128)(2,1)S(1)}, bf16[2,32,512]{1,2,0:T(8,128)(2,1)S(1)}, u32[]{:S(2)}, u32[]{:S(2)}) collective-permute-start(bf16[2,32,512]{1,2,0:T(8,128)(2,1)S(1)} %get-tuple-element.173), channel_id=1, source_target_pairs={{1,0},{2,1},{3,2},{4,3},{5,4},{6,5},{7,6},{8,7},{9,8},{10,9},{11,1... | collective-permute-start | bytes 196616 | tf_op jit(solution)/shard_map/while/body/eval_jaxpr/ppermute | solution.py:18
  54.4 9.8 %collective-permute-start.1 = (bf16[2,32,512]{1,2,0:T(8,128)(2,1)S(1)}, bf16[2,32,512]{1,2,0:T(8,128)(2,1)S(1)}, u32[]{:S(2)}, u32[]{:S(2)}) collective-permute-start(bf16[2,32,512]{1,2,0:T(8,128)(2,1)S(1)} %get-tuple-element.174), channel_id=1, source_target_pairs={{0,1},{1,2},{2,3},{3,4},{4,5},{5,6},{6,7},{7,8},{8,9},{9,10},{10,1... | collective-permute-start | bytes 196616 | tf_op jit(solution)/shard_map/while/body/eval_jaxpr/ppermute | solution.py:15
  64.9 6.8 %collective-permute-start = (bf16[2,32,512]{1,2,0:T(8,128)(2,1)S(1)}, bf16[2,32,512]{1,2,0:T(8,128)(2,1)S(1)}, u32[]{:S(2)}, u32[]{:S(2)}) collective-permute-start(bf16[2,32,512]{1,2,0:T(8,128)(2,1)S(1)} %get-tuple-element.173), channel_id=1, source_target_pairs={{1,0},{2,1},{3,2},{4,3},{5,4},{6,5},{7,6},{8,7},{9,8},{10,9},{11,1... | collective-permute-start | bytes 196616 | tf_op jit(solution)/shard_map/while/body/eval_jaxpr/ppermute | solution.py:18
  66.9 9.8 %collective-permute-start.1 = (bf16[2,32,512]{1,2,0:T(8,128)(2,1)S(1)}, bf16[2,32,512]{1,2,0:T(8,128)(2,1)S(1)}, u32[]{:S(2)}, u32[]{:S(2)}) collective-permute-start(bf16[2,32,512]{1,2,0:T(8,128)(2,1)S(1)} %get-tuple-element.174), channel_id=1, source_target_pairs={{0,1},{1,2},{2,3},{3,4},{4,5},{5,6},{6,7},{7,8},{8,9},{9,10},{10,1... | collective-permute-start | bytes 196616 | tf_op jit(solution)/shard_map/while/body/eval_jaxpr/ppermute | solution.py:15
  77.4 6.8 %collective-permute-start = (bf16[2,32,512]{1,2,0:T(8,128)(2,1)S(1)}, bf16[2,32,512]{1,2,0:T(8,128)(2,1)S(1)}, u32[]{:S(2)}, u32[]{:S(2)}) collective-permute-start(bf16[2,32,512]{1,2,0:T(8,128)(2,1)S(1)} %get-tuple-element.173), channel_id=1, source_target_pairs={{1,0},{2,1},{3,2},{4,3},{5,4},{6,5},{7,6},{8,7},{9,8},{10,9},{11,1... | collective-permute-start | bytes 196616 | tf_op jit(solution)/shard_map/while/body/eval_jaxpr/ppermute | solution.py:18
  79.3 9.9 %collective-permute-start.1 = (bf16[2,32,512]{1,2,0:T(8,128)(2,1)S(1)}, bf16[2,32,512]{1,2,0:T(8,128)(2,1)S(1)}, u32[]{:S(2)}, u32[]{:S(2)}) collective-permute-start(bf16[2,32,512]{1,2,0:T(8,128)(2,1)S(1)} %get-tuple-element.174), channel_id=1, source_target_pairs={{0,1},{1,2},{2,3},{3,4},{4,5},{5,6},{6,7},{7,8},{8,9},{9,10},{10,1... | collective-permute-start | bytes 196616 | tf_op jit(solution)/shard_map/while/body/eval_jaxpr/ppermute | solution.py:15
  89.9 6.8 %collective-permute-start = (bf16[2,32,512]{1,2,0:T(8,128)(2,1)S(1)}, bf16[2,32,512]{1,2,0:T(8,128)(2,1)S(1)}, u32[]{:S(2)}, u32[]{:S(2)}) collective-permute-start(bf16[2,32,512]{1,2,0:T(8,128)(2,1)S(1)} %get-tuple-element.173), channel_id=1, source_target_pairs={{1,0},{2,1},{3,2},{4,3},{5,4},{6,5},{7,6},{8,7},{9,8},{10,9},{11,1... | collective-permute-start | bytes 196616 | tf_op jit(solution)/shard_map/while/body/eval_jaxpr/ppermute | solution.py:18
  91.8 11.2 %collective-permute-start.1 = (bf16[2,32,512]{1,2,0:T(8,128)(2,1)S(1)}, bf16[2,32,512]{1,2,0:T(8,128)(2,1)S(1)}, u32[]{:S(2)}, u32[]{:S(2)}) collective-permute-start(bf16[2,32,512]{1,2,0:T(8,128)(2,1)S(1)} %get-tuple-element.174), channel_id=1, source_target_pairs={{0,1},{1,2},{2,3},{3,4},{4,5},{5,6},{6,7},{7,8},{8,9},{9,10},{10,1... | collective-permute-start | bytes 196616 | tf_op jit(solution)/shard_map/while/body/eval_jaxpr/ppermute | solution.py:15
  103.7 6.8 %collective-permute-start = (bf16[2,32,512]{1,2,0:T(8,128)(2,1)S(1)}, bf16[2,32,512]{1,2,0:T(8,128)(2,1)S(1)}, u32[]{:S(2)}, u32[]{:S(2)}) collective-permute-start(bf16[2,32,512]{1,2,0:T(8,128)(2,1)S(1)} %get-tuple-element.173), channel_id=1, source_target_pairs={{1,0},{2,1},{3,2},{4,3},{5,4},{6,5},{7,6},{8,7},{9,8},{10,9},{11,1... | collective-permute-start | bytes 196616 | tf_op jit(solution)/shard_map/while/body/eval_jaxpr/ppermute | solution.py:18
  105.6 12.5 %collective-permute-start.1 = (bf16[2,32,512]{1,2,0:T(8,128)(2,1)S(1)}, bf16[2,32,512]{1,2,0:T(8,128)(2,1)S(1)}, u32[]{:S(2)}, u32[]{:S(2)}) collective-permute-start(bf16[2,32,512]{1,2,0:T(8,128)(2,1)S(1)} %get-tuple-element.174), channel_id=1, source_target_pairs={{0,1},{1,2},{2,3},{3,4},{4,5},{5,6},{6,7},{7,8},{8,9},{9,10},{10,1... | collective-permute-start | bytes 196616 | tf_op jit(solution)/shard_map/while/body/eval_jaxpr/ppermute | solution.py:15
  118.8 6.8 %collective-permute-start = (bf16[2,32,512]{1,2,0:T(8,128)(2,1)S(1)}, bf16[2,32,512]{1,2,0:T(8,128)(2,1)S(1)}, u32[]{:S(2)}, u32[]{:S(2)}) collective-permute-start(bf16[2,32,512]{1,2,0:T(8,128)(2,1)S(1)} %get-tuple-element.173), channel_id=1, source_target_pairs={{1,0},{2,1},{3,2},{4,3},{5,4},{6,5},{7,6},{8,7},{9,8},{10,9},{11,1... | collective-permute-start | bytes 196616 | tf_op jit(solution)/shard_map/while/body/eval_jaxpr/ppermute | solution.py:18
  120.7 12.5 %collective-permute-start.1 = (bf16[2,32,512]{1,2,0:T(8,128)(2,1)S(1)}, bf16[2,32,512]{1,2,0:T(8,128)(2,1)S(1)}, u32[]{:S(2)}, u32[]{:S(2)}) collective-permute-start(bf16[2,32,512]{1,2,0:T(8,128)(2,1)S(1)} %get-tuple-element.174), channel_id=1, source_target_pairs={{0,1},{1,2},{2,3},{3,4},{4,5},{5,6},{6,7},{7,8},{8,9},{9,10},{10,1... | collective-permute-start | bytes 196616 | tf_op jit(solution)/shard_map/while/body/eval_jaxpr/ppermute | solution.py:15
  134.4 6.5 %collective-permute-start.2 = (bf16[2,32,512]{1,2,0:T(8,128)(2,1)S(1)}, bf16[2,32,512]{1,2,0:T(8,128)(2,1)S(1)}, u32[]{:S(2)}, u32[]{:S(2)}) collective-permute-start(bf16[2,32,512]{1,2,0:T(8,128)(2,1)S(1)} %fusion.64), channel_id=1, source_target_pairs={{1,0},{2,1},{3,2},{4,3},{5,4},{6,5},{7,6},{8,7},{9,8},{10,9},{11,1... | collective-permute-start | bytes 196616 | tf_op jit(solution)/shard_map/while/body/eval_jaxpr/ppermute | solution.py:18
  136.6 12.3 %collective-permute-start.3 = (bf16[2,32,512]{1,2,0:T(8,128)(2,1)S(1)}, bf16[2,32,512]{1,2,0:T(8,128)(2,1)S(1)}, u32[]{:S(2)}, u32[]{:S(2)}) collective-permute-start(bf16[2,32,512]{1,2,0:T(8,128)(2,1)S(1)} %fusion.65), channel_id=1, source_target_pairs={{0,1},{1,2},{2,3},{3,4},{4,5},{5,6},{6,7},{7,8},{8,9},{9,10},{10,1... | collective-permute-start | bytes 196616 | tf_op jit(solution)/shard_map/while/body/eval_jaxpr/ppermute | solution.py:15
  149.6 6.5 %collective-permute-start.2 = (bf16[2,32,512]{1,2,0:T(8,128)(2,1)S(1)}, bf16[2,32,512]{1,2,0:T(8,128)(2,1)S(1)}, u32[]{:S(2)}, u32[]{:S(2)}) collective-permute-start(bf16[2,32,512]{1,2,0:T(8,128)(2,1)S(1)} %fusion.64), channel_id=1, source_target_pairs={{1,0},{2,1},{3,2},{4,3},{5,4},{6,5},{7,6},{8,7},{9,8},{10,9},{11,1... | collective-permute-start | bytes 196616 | tf_op jit(solution)/shard_map/while/body/eval_jaxpr/ppermute | solution.py:18
  151.8 12.0 %collective-permute-start.3 = (bf16[2,32,512]{1,2,0:T(8,128)(2,1)S(1)}, bf16[2,32,512]{1,2,0:T(8,128)(2,1)S(1)}, u32[]{:S(2)}, u32[]{:S(2)}) collective-permute-start(bf16[2,32,512]{1,2,0:T(8,128)(2,1)S(1)} %fusion.65), channel_id=1, source_target_pairs={{0,1},{1,2},{2,3},{3,4},{4,5},{5,6},{6,7},{7,8},{8,9},{9,10},{10,1... | collective-permute-start | bytes 196616 | tf_op jit(solution)/shard_map/while/body/eval_jaxpr/ppermute | solution.py:15
  164.4 6.5 %collective-permute-start.2 = (bf16[2,32,512]{1,2,0:T(8,128)(2,1)S(1)}, bf16[2,32,512]{1,2,0:T(8,128)(2,1)S(1)}, u32[]{:S(2)}, u32[]{:S(2)}) collective-permute-start(bf16[2,32,512]{1,2,0:T(8,128)(2,1)S(1)} %fusion.64), channel_id=1, source_target_pairs={{1,0},{2,1},{3,2},{4,3},{5,4},{6,5},{7,6},{8,7},{9,8},{10,9},{11,1... | collective-permute-start | bytes 196616 | tf_op jit(solution)/shard_map/while/body/eval_jaxpr/ppermute | solution.py:18
  166.6 12.4 %collective-permute-start.3 = (bf16[2,32,512]{1,2,0:T(8,128)(2,1)S(1)}, bf16[2,32,512]{1,2,0:T(8,128)(2,1)S(1)}, u32[]{:S(2)}, u32[]{:S(2)}) collective-permute-start(bf16[2,32,512]{1,2,0:T(8,128)(2,1)S(1)} %fusion.65), channel_id=1, source_target_pairs={{0,1},{1,2},{2,3},{3,4},{4,5},{5,6},{6,7},{7,8},{8,9},{9,10},{10,1... | collective-permute-start | bytes 196616 | tf_op jit(solution)/shard_map/while/body/eval_jaxpr/ppermute | solution.py:15
  179.8 6.5 %collective-permute-start.2 = (bf16[2,32,512]{1,2,0:T(8,128)(2,1)S(1)}, bf16[2,32,512]{1,2,0:T(8,128)(2,1)S(1)}, u32[]{:S(2)}, u32[]{:S(2)}) collective-permute-start(bf16[2,32,512]{1,2,0:T(8,128)(2,1)S(1)} %fusion.64), channel_id=1, source_target_pairs={{1,0},{2,1},{3,2},{4,3},{5,4},{6,5},{7,6},{8,7},{9,8},{10,9},{11,1... | collective-permute-start | bytes 196616 | tf_op jit(solution)/shard_map/while/body/eval_jaxpr/ppermute | solution.py:18
  182.0 12.5 %collective-permute-start.3 = (bf16[2,32,512]{1,2,0:T(8,128)(2,1)S(1)}, bf16[2,32,512]{1,2,0:T(8,128)(2,1)S(1)}, u32[]{:S(2)}, u32[]{:S(2)}) collective-permute-start(bf16[2,32,512]{1,2,0:T(8,128)(2,1)S(1)} %fusion.65), channel_id=1, source_target_pairs={{0,1},{1,2},{2,3},{3,4},{4,5},{5,6},{6,7},{7,8},{8,9},{9,10},{10,1... | collective-permute-start | bytes 196616 | tf_op jit(solution)/shard_map/while/body/eval_jaxpr/ppermute | solution.py:15
  195.1 6.5 %collective-permute-start.2 = (bf16[2,32,512]{1,2,0:T(8,128)(2,1)S(1)}, bf16[2,32,512]{1,2,0:T(8,128)(2,1)S(1)}, u32[]{:S(2)}, u32[]{:S(2)}) collective-permute-start(bf16[2,32,512]{1,2,0:T(8,128)(2,1)S(1)} %fusion.64), channel_id=1, source_target_pairs={{1,0},{2,1},{3,2},{4,3},{5,4},{6,5},{7,6},{8,7},{9,8},{10,9},{11,1... | collective-permute-start | bytes 196616 | tf_op jit(solution)/shard_map/while/body/eval_jaxpr/ppermute | solution.py:18
  197.3 12.5 %collective-permute-start.3 = (bf16[2,32,512]{1,2,0:T(8,128)(2,1)S(1)}, bf16[2,32,512]{1,2,0:T(8,128)(2,1)S(1)}, u32[]{:S(2)}, u32[]{:S(2)}) collective-permute-start(bf16[2,32,512]{1,2,0:T(8,128)(2,1)S(1)} %fusion.65), channel_id=1, source_target_pairs={{0,1},{1,2},{2,3},{3,4},{4,5},{5,6},{6,7},{7,8},{8,9},{9,10},{10,1... | collective-permute-start | bytes 196616 | tf_op jit(solution)/shard_map/while/body/eval_jaxpr/ppermute | solution.py:15
  210.6 6.5 %collective-permute-start.2 = (bf16[2,32,512]{1,2,0:T(8,128)(2,1)S(1)}, bf16[2,32,512]{1,2,0:T(8,128)(2,1)S(1)}, u32[]{:S(2)}, u32[]{:S(2)}) collective-permute-start(bf16[2,32,512]{1,2,0:T(8,128)(2,1)S(1)} %fusion.64), channel_id=1, source_target_pairs={{1,0},{2,1},{3,2},{4,3},{5,4},{6,5},{7,6},{8,7},{9,8},{10,9},{11,1... | collective-permute-start | bytes 196616 | tf_op jit(solution)/shard_map/while/body/eval_jaxpr/ppermute | solution.py:18
  212.8 12.5 %collective-permute-start.3 = (bf16[2,32,512]{1,2,0:T(8,128)(2,1)S(1)}, bf16[2,32,512]{1,2,0:T(8,128)(2,1)S(1)}, u32[]{:S(2)}, u32[]{:S(2)}) collective-permute-start(bf16[2,32,512]{1,2,0:T(8,128)(2,1)S(1)} %fusion.65), channel_id=1, source_target_pairs={{0,1},{1,2},{2,3},{3,4},{4,5},{5,6},{6,7},{7,8},{8,9},{9,10},{10,1... | collective-permute-start | bytes 196616 | tf_op jit(solution)/shard_map/while/body/eval_jaxpr/ppermute | solution.py:15
  226.0 6.5 %collective-permute-start.2 = (bf16[2,32,512]{1,2,0:T(8,128)(2,1)S(1)}, bf16[2,32,512]{1,2,0:T(8,128)(2,1)S(1)}, u32[]{:S(2)}, u32[]{:S(2)}) collective-permute-start(bf16[2,32,512]{1,2,0:T(8,128)(2,1)S(1)} %fusion.64), channel_id=1, source_target_pairs={{1,0},{2,1},{3,2},{4,3},{5,4},{6,5},{7,6},{8,7},{9,8},{10,9},{11,1... | collective-permute-start | bytes 196616 | tf_op jit(solution)/shard_map/while/body/eval_jaxpr/ppermute | solution.py:18
  228.2 12.5 %collective-permute-start.3 = (bf16[2,32,512]{1,2,0:T(8,128)(2,1)S(1)}, bf16[2,32,512]{1,2,0:T(8,128)(2,1)S(1)}, u32[]{:S(2)}, u32[]{:S(2)}) collective-permute-start(bf16[2,32,512]{1,2,0:T(8,128)(2,1)S(1)} %fusion.65), channel_id=1, source_target_pairs={{0,1},{1,2},{2,3},{3,4},{4,5},{5,6},{6,7},{7,8},{8,9},{9,10},{10,1... | collective-permute-start | bytes 196616 | tf_op jit(solution)/shard_map/while/body/eval_jaxpr/ppermute | solution.py:15
  241.4 6.5 %collective-permute-start.2 = (bf16[2,32,512]{1,2,0:T(8,128)(2,1)S(1)}, bf16[2,32,512]{1,2,0:T(8,128)(2,1)S(1)}, u32[]{:S(2)}, u32[]{:S(2)}) collective-permute-start(bf16[2,32,512]{1,2,0:T(8,128)(2,1)S(1)} %fusion.64), channel_id=1, source_target_pairs={{1,0},{2,1},{3,2},{4,3},{5,4},{6,5},{7,6},{8,7},{9,8},{10,9},{11,1... | collective-permute-start | bytes 196616 | tf_op jit(solution)/shard_map/while/body/eval_jaxpr/ppermute | solution.py:18
  243.6 12.5 %collective-permute-start.3 = (bf16[2,32,512]{1,2,0:T(8,128)(2,1)S(1)}, bf16[2,32,512]{1,2,0:T(8,128)(2,1)S(1)}, u32[]{:S(2)}, u32[]{:S(2)}) collective-permute-start(bf16[2,32,512]{1,2,0:T(8,128)(2,1)S(1)} %fusion.65), channel_id=1, source_target_pairs={{0,1},{1,2},{2,3},{3,4},{4,5},{5,6},{6,7},{7,8},{8,9},{9,10},{10,1... | collective-permute-start | bytes 196616 | tf_op jit(solution)/shard_map/while/body/eval_jaxpr/ppermute | solution.py:15
  256.8 6.5 %collective-permute-start.2 = (bf16[2,32,512]{1,2,0:T(8,128)(2,1)S(1)}, bf16[2,32,512]{1,2,0:T(8,128)(2,1)S(1)}, u32[]{:S(2)}, u32[]{:S(2)}) collective-permute-start(bf16[2,32,512]{1,2,0:T(8,128)(2,1)S(1)} %fusion.64), channel_id=1, source_target_pairs={{1,0},{2,1},{3,2},{4,3},{5,4},{6,5},{7,6},{8,7},{9,8},{10,9},{11,1... | collective-permute-start | bytes 196616 | tf_op jit(solution)/shard_map/while/body/eval_jaxpr/ppermute | solution.py:18
  259.0 12.5 %collective-permute-start.3 = (bf16[2,32,512]{1,2,0:T(8,128)(2,1)S(1)}, bf16[2,32,512]{1,2,0:T(8,128)(2,1)S(1)}, u32[]{:S(2)}, u32[]{:S(2)}) collective-permute-start(bf16[2,32,512]{1,2,0:T(8,128)(2,1)S(1)} %fusion.65), channel_id=1, source_target_pairs={{0,1},{1,2},{2,3},{3,4},{4,5},{5,6},{6,7},{7,8},{8,9},{9,10},{10,1... | collective-permute-start | bytes 196616 | tf_op jit(solution)/shard_map/while/body/eval_jaxpr/ppermute | solution.py:15
Sparse Core Ops, SparseCore 0:
  273.2 175.4 all-reduce.1
where the time goes:
time: 459 us; the launch traced here: 457 us
  waiting for transfers between devices  341 us (74%)
  starting transfers between devices  77.9 us (17%)
  matrix products  16.6 us (4%)
  between operations  14.8 us (3%)
  local copies, waits for them, and re-layouts  4.8 us (1%)
    psum x1, waiting for transfers between devices, body(): full = lax.psum(product * (-1.0 / modes), 'energy')  176 us
    ppermute x18, waiting for transfers between devices, with_halo(): lax.ppermute(lax.slice_in_dim(block, block.shape[dim] - width, None, axis...  128 us
    ppermute x18, starting transfers between devices, with_halo(): lax.ppermute(lax.slice_in_dim(block, block.shape[dim] - width, None, axis...  43.3 us
    ppermute x18, waiting for transfers between devices, with_halo(): lax.ppermute(lax.slice_in_dim(block, 0, width, axis=dim), axis, backward)  37.5 us
    ppermute x18, starting transfers between devices, with_halo(): lax.ppermute(lax.slice_in_dim(block, 0, width, axis=dim), axis, backward)  34.7 us
  transfers between devices with their start and end apart: 37, of which 37 were waited for; matrix products, arithmetic and copies ran while one was open for 1% of the time, Pallas kernels for 0%

commit v1 on v0

--- a/solution.py
+++ b/solution.py
@@ -89,7 +89,7 @@
     lam = lax.fori_loop(0, SWEEPS - 1, adjoint_sweep, lam)
     owned = block // lax.axis_size("energy")
     product = jnp.einsum("kim,kjm->ij", lam, psi, preferred_element_type=jnp.float32)
-    full = lax.psum(product * (-1.0 / modes), "energy")
+    full = jnp.sum(lax.all_gather(product * (-1.0 / modes), "energy"), axis=0)
     mine = lax.dynamic_slice_in_dim(full, lax.axis_index("energy") * owned, owned, 0)
     return mine.reshape(1, owned, block)
 

time: 459 us -> 388 us (0.85)
  the two profiles are of different devices: /device:TPU:64 before, /device:TPU:11 now
where the time goes in v1:
time: 388 us; the launch traced here: 384 us
  starting transfers between devices  158 us (41%)
  waiting for transfers between devices  147 us (38%)
  matrix products  55.4 us (14%)
  between operations  14.7 us (4%)
  local copies, waits for them, and re-layouts  4 us (1%)
  other arithmetic  3.94 us (1%)
    ppermute x18, starting transfers between devices, with_halo(): lax.ppermute(lax.slice_in_dim(block, 0, width, axis=dim), axis, backward)  119 us
    all_gather x1, waiting for transfers between devices, body(): full = jnp.sum(lax.all_gather(product * (-1.0 / modes), 'energy'), axis=0)  86.8 us
    ppermute x18, waiting for transfers between devices, with_halo(): lax.ppermute(lax.slice_in_dim(block, block.shape[dim] - width, None, axis...  40.9 us
    ppermute x18, starting transfers between devices, with_halo(): lax.ppermute(lax.slice_in_dim(block, block.shape[dim] - width, None, axis...  39.4 us
    ppermute x18, waiting for transfers between devices, with_halo(): lax.ppermute(lax.slice_in_dim(block, 0, width, axis=dim), axis, backward)  18.9 us
    dot_general x9, matrix products, forward_sweep(): jnp.einsum('kij,kjm->kim', inverse_blocks, rhs, preferred_element_type=jn...  13.3 us
    dot_general x9, matrix products, adjoint_sweep(): jnp.einsum('kji,kjm->kim', inverse_blocks, update, preferred_element_type...  11.9 us
    dot_general x9, matrix products, adjoint_sweep(): jnp.einsum('ei,kim->kem', left_coupling, lam, preferred_element_type=jnp....  8.86 us
  transfers between devices with their start and end apart: 37, of which 28 were waited for; matrix products, arithmetic and copies ran while one was open for 5% of the time, Pallas kernels for 0%

profile of v1, /device:TPU:11, one launch (start us, length us, event | category | flops | bytes accessed | tf_op | source)
XLA Modules:
  0.0 383.9 jit_solution(14339001861566698999)
XLA Ops:
  11.5 129.7 %while.20 = (s32[]{:T(128)}, bf16[2,256,512]{1,2,0:T(8,128)(2,1)S(1)}, bf16[2,256,512]{1,2,0:T(8,128)(2,1)S(1)}, bf16[32,256]{1,0:T(8,128)(2,1)}, bf16[32,256]{1...) while((s32[]{:T(128)}, bf16[2,256,512]{1,2,0:T(8,128)(2,1)S(1)}, ...), condition=%wide.region_1.0_spmd, body=%wide.region_0.0_spmd.sunk | while | flops 169082880 | bytes 4358301 | solution.py:56
  11.6 2.6 collective-permute-start
  14.2 3.9 %collective-permute-start.1 = (bf16[2,32,512]{1,2,0:T(8,128)(2,1)S(1)}, bf16[2,32,512]{1,2,0:T(8,128)(2,1)S(1)}, u32[]{:S(2)}, u32[]{:S(2)}) collective-permute-start(bf16[2,32,512]{1,2,0:T(8,128)(2,1)S(1)} %get-tuple-element.174), channel_id=1, source_target_pairs={{0,1},{1,2},{2,3},{3,4},{4,5},{5,6},{6,7},{7,8},{8,9},{9,10},{10,1... | collective-permute-start | bytes 196616 | tf_op jit(solution)/shard_map/while/body/eval_jaxpr/ppermute | solution.py:15
  18.1 2.1 collective-permute-done
  23.0 2.4 collective-permute-start
  25.5 4.8 %collective-permute-start.1 = (bf16[2,32,512]{1,2,0:T(8,128)(2,1)S(1)}, bf16[2,32,512]{1,2,0:T(8,128)(2,1)S(1)}, u32[]{:S(2)}, u32[]{:S(2)}) collective-permute-start(bf16[2,32,512]{1,2,0:T(8,128)(2,1)S(1)} %get-tuple-element.174), channel_id=1, source_target_pairs={{0,1},{1,2},{2,3},{3,4},{4,5},{5,6},{6,7},{7,8},{8,9},{9,10},{10,1... | collective-permute-start | bytes 196616 | tf_op jit(solution)/shard_map/while/body/eval_jaxpr/ppermute | solution.py:15
  30.2 2.9 collective-permute-done
  34.1 1.6 collective-permute-done.1
  37.4 10.8 %collective-permute-start = (bf16[2,32,512]{1,2,0:T(8,128)(2,1)S(1)}, bf16[2,32,512]{1,2,0:T(8,128)(2,1)S(1)}, u32[]{:S(2)}, u32[]{:S(2)}) collective-permute-start(bf16[2,32,512]{1,2,0:T(8,128)(2,1)S(1)} %get-tuple-element.173), channel_id=1, source_target_pairs={{1,0},{2,1},{3,2},{4,3},{5,4},{6,5},{7,6},{8,7},{9,8},{10,9},{11,1... | collective-permute-start | bytes 196616 | tf_op jit(solution)/shard_map/while/body/eval_jaxpr/ppermute | solution.py:18
  48.2 1.9 collective-permute-start.1
  51.1 3.4 collective-permute-done.1
  54.5 1.5 fusion.57
  56.1 5.5 %collective-permute-start = (bf16[2,32,512]{1,2,0:T(8,128)(2,1)S(1)}, bf16[2,32,512]{1,2,0:T(8,128)(2,1)S(1)}, u32[]{:S(2)}, u32[]{:S(2)}) collective-permute-start(bf16[2,32,512]{1,2,0:T(8,128)(2,1)S(1)} %get-tuple-element.173), channel_id=1, source_target_pairs={{1,0},{2,1},{3,2},{4,3},{5,4},{6,5},{7,6},{8,7},{9,8},{10,9},{11,1... | collective-permute-start | bytes 196616 | tf_op jit(solution)/shard_map/while/body/eval_jaxpr/ppermute | solution.py:18
  61.6 1.9 collective-permute-start.1
  63.6 2.9 collective-permute-done
  69.6 5.6 %collective-permute-start = (bf16[2,32,512]{1,2,0:T(8,128)(2,1)S(1)}, bf16[2,32,512]{1,2,0:T(8,128)(2,1)S(1)}, u32[]{:S(2)}, u32[]{:S(2)}) collective-permute-start(bf16[2,32,512]{1,2,0:T(8,128)(2,1)S(1)} %get-tuple-element.173), channel_id=1, source_target_pairs={{1,0},{2,1},{3,2},{4,3},{5,4},{6,5},{7,6},{8,7},{9,8},{10,9},{11,1... | collective-permute-start | bytes 196616 | tf_op jit(solution)/shard_map/while/body/eval_jaxpr/ppermute | solution.py:18
  75.2 1.9 collective-permute-start.1
  77.1 2.8 collective-permute-done
  81.5 1.5 fusion.57
  83.1 5.6 %collective-permute-start = (bf16[2,32,512]{1,2,0:T(8,128)(2,1)S(1)}, bf16[2,32,512]{1,2,0:T(8,128)(2,1)S(1)}, u32[]{:S(2)}, u32[]{:S(2)}) collective-permute-start(bf16[2,32,512]{1,2,0:T(8,128)(2,1)S(1)} %get-tuple-element.173), channel_id=1, source_target_pairs={{1,0},{2,1},{3,2},{4,3},{5,4},{6,5},{7,6},{8,7},{9,8},{10,9},{11,1... | collective-permute-start | bytes 196616 | tf_op jit(solution)/shard_map/while/body/eval_jaxpr/ppermute | solution.py:18
  88.7 1.9 collective-permute-start.1
  90.7 2.8 collective-permute-done
  95.0 1.5 fusion.57
  96.7 6.2 %collective-permute-start = (bf16[2,32,512]{1,2,0:T(8,128)(2,1)S(1)}, bf16[2,32,512]{1,2,0:T(8,128)(2,1)S(1)}, u32[]{:S(2)}, u32[]{:S(2)}) collective-permute-start(bf16[2,32,512]{1,2,0:T(8,128)(2,1)S(1)} %get-tuple-element.173), channel_id=1, source_target_pairs={{1,0},{2,1},{3,2},{4,3},{5,4},{6,5},{7,6},{8,7},{9,8},{10,9},{11,1... | collective-permute-start | bytes 196616 | tf_op jit(solution)/shard_map/while/body/eval_jaxpr/ppermute | solution.py:18
  102.9 1.9 collective-permute-start.1
  104.8 2.2 collective-permute-done
  110.8 7.2 %collective-permute-start = (bf16[2,32,512]{1,2,0:T(8,128)(2,1)S(1)}, bf16[2,32,512]{1,2,0:T(8,128)(2,1)S(1)}, u32[]{:S(2)}, u32[]{:S(2)}) collective-permute-start(bf16[2,32,512]{1,2,0:T(8,128)(2,1)S(1)} %get-tuple-element.173), channel_id=1, source_target_pairs={{1,0},{2,1},{3,2},{4,3},{5,4},{6,5},{7,6},{8,7},{9,8},{10,9},{11,1... | collective-permute-start | bytes 196616 | tf_op jit(solution)/shard_map/while/body/eval_jaxpr/ppermute | solution.py:18
  118.0 1.9 collective-permute-start.1
  122.2 2.1 collective-permute-done.1
  124.3 1.5 fusion.57
  125.9 7.4 %collective-permute-start = (bf16[2,32,512]{1,2,0:T(8,128)(2,1)S(1)}, bf16[2,32,512]{1,2,0:T(8,128)(2,1)S(1)}, u32[]{:S(2)}, u32[]{:S(2)}) collective-permute-start(bf16[2,32,512]{1,2,0:T(8,128)(2,1)S(1)} %get-tuple-element.173), channel_id=1, source_target_pairs={{1,0},{2,1},{3,2},{4,3},{5,4},{6,5},{7,6},{8,7},{9,8},{10,9},{11,1... | collective-permute-start | bytes 196616 | tf_op jit(solution)/shard_map/while/body/eval_jaxpr/ppermute | solution.py:18
  133.4 1.9 collective-permute-start.1
  137.2 2.4 collective-permute-done.1
  139.7 1.5 fusion.57
  142.5 143.6 %while.21 = (s32[]{:T(128)}, bf16[2,256,512]{1,2,0:T(8,128)(2,1)S(1)}, bf16[32,256]{1,0:T(8,128)(2,1)}, bf16[32,256]{1,0:T(8,128)(2,1)}, f32[2,256,512]{1,2,0:T(...) while((s32[]{:T(128)}, bf16[2,256,512]{1,2,0:T(8,128)(2,1)S(1)}, ...), condition=%wide.region_3.0_spmd, body=%wide.region_2.0_spmd.sunk | while | flops 169213952 | bytes 4230837 | solution.py:89
  143.5 7.4 %collective-permute-start.2 = (bf16[2,32,512]{1,2,0:T(8,128)(2,1)S(1)}, bf16[2,32,512]{1,2,0:T(8,128)(2,1)S(1)}, u32[]{:S(2)}, u32[]{:S(2)}) collective-permute-start(bf16[2,32,512]{1,2,0:T(8,128)(2,1)S(1)} %fusion.64), channel_id=1, source_target_pairs={{1,0},{2,1},{3,2},{4,3},{5,4},{6,5},{7,6},{8,7},{9,8},{10,9},{11,1... | collective-permute-start | bytes 196616 | tf_op jit(solution)/shard_map/while/body/eval_jaxpr/ppermute | solution.py:18
  152.0 1.9 collective-permute-start.3
  154.0 3.3 collective-permute-done.3
  159.6 5.5 %collective-permute-start.2 = (bf16[2,32,512]{1,2,0:T(8,128)(2,1)S(1)}, bf16[2,32,512]{1,2,0:T(8,128)(2,1)S(1)}, u32[]{:S(2)}, u32[]{:S(2)}) collective-permute-start(bf16[2,32,512]{1,2,0:T(8,128)(2,1)S(1)} %fusion.64), channel_id=1, source_target_pairs={{1,0},{2,1},{3,2},{4,3},{5,4},{6,5},{7,6},{8,7},{9,8},{10,9},{11,1... | collective-permute-start | bytes 196616 | tf_op jit(solution)/shard_map/while/body/eval_jaxpr/ppermute | solution.py:18
  166.1 1.9 collective-permute-start.3
  169.0 2.4 collective-permute-done.3
  173.8 6.9 %collective-permute-start.2 = (bf16[2,32,512]{1,2,0:T(8,128)(2,1)S(1)}, bf16[2,32,512]{1,2,0:T(8,128)(2,1)S(1)}, u32[]{:S(2)}, u32[]{:S(2)}) collective-permute-start(bf16[2,32,512]{1,2,0:T(8,128)(2,1)S(1)} %fusion.64), channel_id=1, source_target_pairs={{1,0},{2,1},{3,2},{4,3},{5,4},{6,5},{7,6},{8,7},{9,8},{10,9},{11,1... | collective-permute-start | bytes 196616 | tf_op jit(solution)/shard_map/while/body/eval_jaxpr/ppermute | solution.py:18
  181.7 1.9 collective-permute-start.3
  183.7 3.3 collective-permute-done.3
  189.3 7.6 %collective-permute-start.2 = (bf16[2,32,512]{1,2,0:T(8,128)(2,1)S(1)}, bf16[2,32,512]{1,2,0:T(8,128)(2,1)S(1)}, u32[]{:S(2)}, u32[]{:S(2)}) collective-permute-start(bf16[2,32,512]{1,2,0:T(8,128)(2,1)S(1)} %fusion.64), channel_id=1, source_target_pairs={{1,0},{2,1},{3,2},{4,3},{5,4},{6,5},{7,6},{8,7},{9,8},{10,9},{11,1... | collective-permute-start | bytes 196616 | tf_op jit(solution)/shard_map/while/body/eval_jaxpr/ppermute | solution.py:18
  198.0 1.9 collective-permute-start.3
  200.0 3.3 collective-permute-done.3
  205.6 7.6 %collective-permute-start.2 = (bf16[2,32,512]{1,2,0:T(8,128)(2,1)S(1)}, bf16[2,32,512]{1,2,0:T(8,128)(2,1)S(1)}, u32[]{:S(2)}, u32[]{:S(2)}) collective-permute-start(bf16[2,32,512]{1,2,0:T(8,128)(2,1)S(1)} %fusion.64), channel_id=1, source_target_pairs={{1,0},{2,1},{3,2},{4,3},{5,4},{6,5},{7,6},{8,7},{9,8},{10,9},{11,1... | collective-permute-start | bytes 196616 | tf_op jit(solution)/shard_map/while/body/eval_jaxpr/ppermute | solution.py:18
  214.2 1.9 collective-permute-start.3
  216.3 3.3 collective-permute-done.3
  221.9 7.6 %collective-permute-start.2 = (bf16[2,32,512]{1,2,0:T(8,128)(2,1)S(1)}, bf16[2,32,512]{1,2,0:T(8,128)(2,1)S(1)}, u32[]{:S(2)}, u32[]{:S(2)}) collective-permute-start(bf16[2,32,512]{1,2,0:T(8,128)(2,1)S(1)} %fusion.64), channel_id=1, source_target_pairs={{1,0},{2,1},{3,2},{4,3},{5,4},{6,5},{7,6},{8,7},{9,8},{10,9},{11,1... | collective-permute-start | bytes 196616 | tf_op jit(solution)/shard_map/while/body/eval_jaxpr/ppermute | solution.py:18
  230.6 1.9 collective-permute-start.3
  232.6 3.3 collective-permute-done.3
  238.2 7.6 %collective-permute-start.2 = (bf16[2,32,512]{1,2,0:T(8,128)(2,1)S(1)}, bf16[2,32,512]{1,2,0:T(8,128)(2,1)S(1)}, u32[]{:S(2)}, u32[]{:S(2)}) collective-permute-start(bf16[2,32,512]{1,2,0:T(8,128)(2,1)S(1)} %fusion.64), channel_id=1, source_target_pairs={{1,0},{2,1},{3,2},{4,3},{5,4},{6,5},{7,6},{8,7},{9,8},{10,9},{11,1... | collective-permute-start | bytes 196616 | tf_op jit(solution)/shard_map/while/body/eval_jaxpr/ppermute | solution.py:18
  246.8 1.9 collective-permute-start.3
  248.9 3.2 collective-permute-done.3
  254.5 7.6 %collective-permute-start.2 = (bf16[2,32,512]{1,2,0:T(8,128)(2,1)S(1)}, bf16[2,32,512]{1,2,0:T(8,128)(2,1)S(1)}, u32[]{:S(2)}, u32[]{:S(2)}) collective-permute-start(bf16[2,32,512]{1,2,0:T(8,128)(2,1)S(1)} %fusion.64), channel_id=1, source_target_pairs={{1,0},{2,1},{3,2},{4,3},{5,4},{6,5},{7,6},{8,7},{9,8},{10,9},{11,1... | collective-permute-start | bytes 196616 | tf_op jit(solution)/shard_map/while/body/eval_jaxpr/ppermute | solution.py:18
  263.1 1.9 collective-permute-start.3
  265.2 3.2 collective-permute-done.3
  270.8 7.6 %collective-permute-start.2 = (bf16[2,32,512]{1,2,0:T(8,128)(2,1)S(1)}, bf16[2,32,512]{1,2,0:T(8,128)(2,1)S(1)}, u32[]{:S(2)}, u32[]{:S(2)}) collective-permute-start(bf16[2,32,512]{1,2,0:T(8,128)(2,1)S(1)} %fusion.64), channel_id=1, source_target_pairs={{1,0},{2,1},{3,2},{4,3},{5,4},{6,5},{7,6},{8,7},{9,8},{10,9},{11,1... | collective-permute-start | bytes 196616 | tf_op jit(solution)/shard_map/while/body/eval_jaxpr/ppermute | solution.py:18
  279.4 1.9 collective-permute-start.3
  281.5 3.3 collective-permute-done.3
  287.2 86.8 %all-gather.3.cloned.1.call-done = f32[4096,256]{1,0:T(8,128)} async-done(((f32[256,256]{1,0:T(8,128)}), f32[4096,256]{1,0:T(8,128)}) %all-gather.3.cloned.1.call-update) | async-done | bytes 4194320 | tf_op jit(solution)/shard_map/all_gather | solution.py:92
  374.0 2.5 reduce_sum.9
  (114 shorter events, 59.5 us)
Async XLA Ops:
  6.5 367.5 %all-gather.3.cloned.1.call-start = ((), (), s32[]{:S(2)}) async-start(), calls=%async_computation | async-start | bytes 4456448 | tf_op jit(solution)/shard_map/all_gather | solution.py:92
  11.6 8.6 %collective-permute-start = (bf16[2,32,512]{1,2,0:T(8,128)(2,1)S(1)}, bf16[2,32,512]{1,2,0:T(8,128)(2,1)S(1)}, u32[]{:S(2)}, u32[]{:S(2)}) collective-permute-start(bf16[2,32,512]{1,2,0:T(8,128)(2,1)S(1)} %get-tuple-element.173), channel_id=1, source_target_pairs={{1,0},{2,1},{3,2},{4,3},{5,4},{6,5},{7,6},{8,7},{9,8},{10,9},{11,1... | collective-permute-start | bytes 196616 | tf_op jit(solution)/shard_map/while/body/eval_jaxpr/ppermute | solution.py:18
  14.2 7.2 %collective-permute-start.1 = (bf16[2,32,512]{1,2,0:T(8,128)(2,1)S(1)}, bf16[2,32,512]{1,2,0:T(8,128)(2,1)S(1)}, u32[]{:S(2)}, u32[]{:S(2)}) collective-permute-start(bf16[2,32,512]{1,2,0:T(8,128)(2,1)S(1)} %get-tuple-element.174), channel_id=1, source_target_pairs={{0,1},{1,2},{2,3},{3,4},{4,5},{5,6},{6,7},{7,8},{8,9},{9,10},{10,1... | collective-permute-start | bytes 196616 | tf_op jit(solution)/shard_map/while/body/eval_jaxpr/ppermute | solution.py:15
  23.0 10.1 %collective-permute-start = (bf16[2,32,512]{1,2,0:T(8,128)(2,1)S(1)}, bf16[2,32,512]{1,2,0:T(8,128)(2,1)S(1)}, u32[]{:S(2)}, u32[]{:S(2)}) collective-permute-start(bf16[2,32,512]{1,2,0:T(8,128)(2,1)S(1)} %get-tuple-element.173), channel_id=1, source_target_pairs={{1,0},{2,1},{3,2},{4,3},{5,4},{6,5},{7,6},{8,7},{9,8},{10,9},{11,1... | collective-permute-start | bytes 196616 | tf_op jit(solution)/shard_map/while/body/eval_jaxpr/ppermute | solution.py:18
  25.5 10.3 %collective-permute-start.1 = (bf16[2,32,512]{1,2,0:T(8,128)(2,1)S(1)}, bf16[2,32,512]{1,2,0:T(8,128)(2,1)S(1)}, u32[]{:S(2)}, u32[]{:S(2)}) collective-permute-start(bf16[2,32,512]{1,2,0:T(8,128)(2,1)S(1)} %get-tuple-element.174), channel_id=1, source_target_pairs={{0,1},{1,2},{2,3},{3,4},{4,5},{5,6},{6,7},{7,8},{8,9},{9,10},{10,1... | collective-permute-start | bytes 196616 | tf_op jit(solution)/shard_map/while/body/eval_jaxpr/ppermute | solution.py:15
  37.4 12.8 %collective-permute-start = (bf16[2,32,512]{1,2,0:T(8,128)(2,1)S(1)}, bf16[2,32,512]{1,2,0:T(8,128)(2,1)S(1)}, u32[]{:S(2)}, u32[]{:S(2)}) collective-permute-start(bf16[2,32,512]{1,2,0:T(8,128)(2,1)S(1)} %get-tuple-element.173), channel_id=1, source_target_pairs={{1,0},{2,1},{3,2},{4,3},{5,4},{6,5},{7,6},{8,7},{9,8},{10,9},{11,1... | collective-permute-start | bytes 196616 | tf_op jit(solution)/shard_map/while/body/eval_jaxpr/ppermute | solution.py:18
  48.2 6.3 %collective-permute-start.1 = (bf16[2,32,512]{1,2,0:T(8,128)(2,1)S(1)}, bf16[2,32,512]{1,2,0:T(8,128)(2,1)S(1)}, u32[]{:S(2)}, u32[]{:S(2)}) collective-permute-start(bf16[2,32,512]{1,2,0:T(8,128)(2,1)S(1)} %get-tuple-element.174), channel_id=1, source_target_pairs={{0,1},{1,2},{2,3},{3,4},{4,5},{5,6},{6,7},{7,8},{8,9},{9,10},{10,1... | collective-permute-start | bytes 196616 | tf_op jit(solution)/shard_map/while/body/eval_jaxpr/ppermute | solution.py:15
  56.1 10.3 %collective-permute-start = (bf16[2,32,512]{1,2,0:T(8,128)(2,1)S(1)}, bf16[2,32,512]{1,2,0:T(8,128)(2,1)S(1)}, u32[]{:S(2)}, u32[]{:S(2)}) collective-permute-start(bf16[2,32,512]{1,2,0:T(8,128)(2,1)S(1)} %get-tuple-element.173), channel_id=1, source_target_pairs={{1,0},{2,1},{3,2},{4,3},{5,4},{6,5},{7,6},{8,7},{9,8},{10,9},{11,1... | collective-permute-start | bytes 196616 | tf_op jit(solution)/shard_map/while/body/eval_jaxpr/ppermute | solution.py:18
  61.6 6.3 %collective-permute-start.1 = (bf16[2,32,512]{1,2,0:T(8,128)(2,1)S(1)}, bf16[2,32,512]{1,2,0:T(8,128)(2,1)S(1)}, u32[]{:S(2)}, u32[]{:S(2)}) collective-permute-start(bf16[2,32,512]{1,2,0:T(8,128)(2,1)S(1)} %get-tuple-element.174), channel_id=1, source_target_pairs={{0,1},{1,2},{2,3},{3,4},{4,5},{5,6},{6,7},{7,8},{8,9},{9,10},{10,1... | collective-permute-start | bytes 196616 | tf_op jit(solution)/shard_map/while/body/eval_jaxpr/ppermute | solution.py:15
  69.6 10.3 %collective-permute-start = (bf16[2,32,512]{1,2,0:T(8,128)(2,1)S(1)}, bf16[2,32,512]{1,2,0:T(8,128)(2,1)S(1)}, u32[]{:S(2)}, u32[]{:S(2)}) collective-permute-start(bf16[2,32,512]{1,2,0:T(8,128)(2,1)S(1)} %get-tuple-element.173), channel_id=1, source_target_pairs={{1,0},{2,1},{3,2},{4,3},{5,4},{6,5},{7,6},{8,7},{9,8},{10,9},{11,1... | collective-permute-start | bytes 196616 | tf_op jit(solution)/shard_map/while/body/eval_jaxpr/ppermute | solution.py:18
  75.2 6.3 %collective-permute-start.1 = (bf16[2,32,512]{1,2,0:T(8,128)(2,1)S(1)}, bf16[2,32,512]{1,2,0:T(8,128)(2,1)S(1)}, u32[]{:S(2)}, u32[]{:S(2)}) collective-permute-start(bf16[2,32,512]{1,2,0:T(8,128)(2,1)S(1)} %get-tuple-element.174), channel_id=1, source_target_pairs={{0,1},{1,2},{2,3},{3,4},{4,5},{5,6},{6,7},{7,8},{8,9},{9,10},{10,1... | collective-permute-start | bytes 196616 | tf_op jit(solution)/shard_map/while/body/eval_jaxpr/ppermute | solution.py:15
  83.1 10.3 %collective-permute-start = (bf16[2,32,512]{1,2,0:T(8,128)(2,1)S(1)}, bf16[2,32,512]{1,2,0:T(8,128)(2,1)S(1)}, u32[]{:S(2)}, u32[]{:S(2)}) collective-permute-start(bf16[2,32,512]{1,2,0:T(8,128)(2,1)S(1)} %get-tuple-element.173), channel_id=1, source_target_pairs={{1,0},{2,1},{3,2},{4,3},{5,4},{6,5},{7,6},{8,7},{9,8},{10,9},{11,1... | collective-permute-start | bytes 196616 | tf_op jit(solution)/shard_map/while/body/eval_jaxpr/ppermute | solution.py:18
  88.7 6.3 %collective-permute-start.1 = (bf16[2,32,512]{1,2,0:T(8,128)(2,1)S(1)}, bf16[2,32,512]{1,2,0:T(8,128)(2,1)S(1)}, u32[]{:S(2)}, u32[]{:S(2)}) collective-permute-start(bf16[2,32,512]{1,2,0:T(8,128)(2,1)S(1)} %get-tuple-element.174), channel_id=1, source_target_pairs={{0,1},{1,2},{2,3},{3,4},{4,5},{5,6},{6,7},{7,8},{8,9},{9,10},{10,1... | collective-permute-start | bytes 196616 | tf_op jit(solution)/shard_map/while/body/eval_jaxpr/ppermute | solution.py:15
  96.7 10.3 %collective-permute-start = (bf16[2,32,512]{1,2,0:T(8,128)(2,1)S(1)}, bf16[2,32,512]{1,2,0:T(8,128)(2,1)S(1)}, u32[]{:S(2)}, u32[]{:S(2)}) collective-permute-start(bf16[2,32,512]{1,2,0:T(8,128)(2,1)S(1)} %get-tuple-element.173), channel_id=1, source_target_pairs={{1,0},{2,1},{3,2},{4,3},{5,4},{6,5},{7,6},{8,7},{9,8},{10,9},{11,1... | collective-permute-start | bytes 196616 | tf_op jit(solution)/shard_map/while/body/eval_jaxpr/ppermute | solution.py:18
  102.9 6.3 %collective-permute-start.1 = (bf16[2,32,512]{1,2,0:T(8,128)(2,1)S(1)}, bf16[2,32,512]{1,2,0:T(8,128)(2,1)S(1)}, u32[]{:S(2)}, u32[]{:S(2)}) collective-permute-start(bf16[2,32,512]{1,2,0:T(8,128)(2,1)S(1)} %get-tuple-element.174), channel_id=1, source_target_pairs={{0,1},{1,2},{2,3},{3,4},{4,5},{5,6},{6,7},{7,8},{8,9},{9,10},{10,1... | collective-permute-start | bytes 196616 | tf_op jit(solution)/shard_map/while/body/eval_jaxpr/ppermute | solution.py:15
  110.8 10.3 %collective-permute-start = (bf16[2,32,512]{1,2,0:T(8,128)(2,1)S(1)}, bf16[2,32,512]{1,2,0:T(8,128)(2,1)S(1)}, u32[]{:S(2)}, u32[]{:S(2)}) collective-permute-start(bf16[2,32,512]{1,2,0:T(8,128)(2,1)S(1)} %get-tuple-element.173), channel_id=1, source_target_pairs={{1,0},{2,1},{3,2},{4,3},{5,4},{6,5},{7,6},{8,7},{9,8},{10,9},{11,1... | collective-permute-start | bytes 196616 | tf_op jit(solution)/shard_map/while/body/eval_jaxpr/ppermute | solution.py:18
  118.0 6.3 %collective-permute-start.1 = (bf16[2,32,512]{1,2,0:T(8,128)(2,1)S(1)}, bf16[2,32,512]{1,2,0:T(8,128)(2,1)S(1)}, u32[]{:S(2)}, u32[]{:S(2)}) collective-permute-start(bf16[2,32,512]{1,2,0:T(8,128)(2,1)S(1)} %get-tuple-element.174), channel_id=1, source_target_pairs={{0,1},{1,2},{2,3},{3,4},{4,5},{5,6},{6,7},{7,8},{8,9},{9,10},{10,1... | collective-permute-start | bytes 196616 | tf_op jit(solution)/shard_map/while/body/eval_jaxpr/ppermute | solution.py:15
  125.9 10.3 %collective-permute-start = (bf16[2,32,512]{1,2,0:T(8,128)(2,1)S(1)}, bf16[2,32,512]{1,2,0:T(8,128)(2,1)S(1)}, u32[]{:S(2)}, u32[]{:S(2)}) collective-permute-start(bf16[2,32,512]{1,2,0:T(8,128)(2,1)S(1)} %get-tuple-element.173), channel_id=1, source_target_pairs={{1,0},{2,1},{3,2},{4,3},{5,4},{6,5},{7,6},{8,7},{9,8},{10,9},{11,1... | collective-permute-start | bytes 196616 | tf_op jit(solution)/shard_map/while/body/eval_jaxpr/ppermute | solution.py:18
  133.4 6.3 %collective-permute-start.1 = (bf16[2,32,512]{1,2,0:T(8,128)(2,1)S(1)}, bf16[2,32,512]{1,2,0:T(8,128)(2,1)S(1)}, u32[]{:S(2)}, u32[]{:S(2)}) collective-permute-start(bf16[2,32,512]{1,2,0:T(8,128)(2,1)S(1)} %get-tuple-element.174), channel_id=1, source_target_pairs={{0,1},{1,2},{2,3},{3,4},{4,5},{5,6},{6,7},{7,8},{8,9},{9,10},{10,1... | collective-permute-start | bytes 196616 | tf_op jit(solution)/shard_map/while/body/eval_jaxpr/ppermute | solution.py:15
  143.5 10.5 %collective-permute-start.2 = (bf16[2,32,512]{1,2,0:T(8,128)(2,1)S(1)}, bf16[2,32,512]{1,2,0:T(8,128)(2,1)S(1)}, u32[]{:S(2)}, u32[]{:S(2)}) collective-permute-start(bf16[2,32,512]{1,2,0:T(8,128)(2,1)S(1)} %fusion.64), channel_id=1, source_target_pairs={{1,0},{2,1},{3,2},{4,3},{5,4},{6,5},{7,6},{8,7},{9,8},{10,9},{11,1... | collective-permute-start | bytes 196616 | tf_op jit(solution)/shard_map/while/body/eval_jaxpr/ppermute | solution.py:18
  152.0 5.3 %collective-permute-start.3 = (bf16[2,32,512]{1,2,0:T(8,128)(2,1)S(1)}, bf16[2,32,512]{1,2,0:T(8,128)(2,1)S(1)}, u32[]{:S(2)}, u32[]{:S(2)}) collective-permute-start(bf16[2,32,512]{1,2,0:T(8,128)(2,1)S(1)} %fusion.65), channel_id=1, source_target_pairs={{0,1},{1,2},{2,3},{3,4},{4,5},{5,6},{6,7},{7,8},{8,9},{9,10},{10,1... | collective-permute-start | bytes 196616 | tf_op jit(solution)/shard_map/while/body/eval_jaxpr/ppermute | solution.py:15
  159.6 9.4 %collective-permute-start.2 = (bf16[2,32,512]{1,2,0:T(8,128)(2,1)S(1)}, bf16[2,32,512]{1,2,0:T(8,128)(2,1)S(1)}, u32[]{:S(2)}, u32[]{:S(2)}) collective-permute-start(bf16[2,32,512]{1,2,0:T(8,128)(2,1)S(1)} %fusion.64), channel_id=1, source_target_pairs={{1,0},{2,1},{3,2},{4,3},{5,4},{6,5},{7,6},{8,7},{9,8},{10,9},{11,1... | collective-permute-start | bytes 196616 | tf_op jit(solution)/shard_map/while/body/eval_jaxpr/ppermute | solution.py:18
  166.1 5.3 %collective-permute-start.3 = (bf16[2,32,512]{1,2,0:T(8,128)(2,1)S(1)}, bf16[2,32,512]{1,2,0:T(8,128)(2,1)S(1)}, u32[]{:S(2)}, u32[]{:S(2)}) collective-permute-start(bf16[2,32,512]{1,2,0:T(8,128)(2,1)S(1)} %fusion.65), channel_id=1, source_target_pairs={{0,1},{1,2},{2,3},{3,4},{4,5},{5,6},{6,7},{7,8},{8,9},{9,10},{10,1... | collective-permute-start | bytes 196616 | tf_op jit(solution)/shard_map/while/body/eval_jaxpr/ppermute | solution.py:15
  173.8 9.9 %collective-permute-start.2 = (bf16[2,32,512]{1,2,0:T(8,128)(2,1)S(1)}, bf16[2,32,512]{1,2,0:T(8,128)(2,1)S(1)}, u32[]{:S(2)}, u32[]{:S(2)}) collective-permute-start(bf16[2,32,512]{1,2,0:T(8,128)(2,1)S(1)} %fusion.64), channel_id=1, source_target_pairs={{1,0},{2,1},{3,2},{4,3},{5,4},{6,5},{7,6},{8,7},{9,8},{10,9},{11,1... | collective-permute-start | bytes 196616 | tf_op jit(solution)/shard_map/while/body/eval_jaxpr/ppermute | solution.py:18
  181.7 5.3 %collective-permute-start.3 = (bf16[2,32,512]{1,2,0:T(8,128)(2,1)S(1)}, bf16[2,32,512]{1,2,0:T(8,128)(2,1)S(1)}, u32[]{:S(2)}, u32[]{:S(2)}) collective-permute-start(bf16[2,32,512]{1,2,0:T(8,128)(2,1)S(1)} %fusion.65), channel_id=1, source_target_pairs={{0,1},{1,2},{2,3},{3,4},{4,5},{5,6},{6,7},{7,8},{8,9},{9,10},{10,1... | collective-permute-start | bytes 196616 | tf_op jit(solution)/shard_map/while/body/eval_jaxpr/ppermute | solution.py:15
  189.3 10.6 %collective-permute-start.2 = (bf16[2,32,512]{1,2,0:T(8,128)(2,1)S(1)}, bf16[2,32,512]{1,2,0:T(8,128)(2,1)S(1)}, u32[]{:S(2)}, u32[]{:S(2)}) collective-permute-start(bf16[2,32,512]{1,2,0:T(8,128)(2,1)S(1)} %fusion.64), channel_id=1, source_target_pairs={{1,0},{2,1},{3,2},{4,3},{5,4},{6,5},{7,6},{8,7},{9,8},{10,9},{11,1... | collective-permute-start | bytes 196616 | tf_op jit(solution)/shard_map/while/body/eval_jaxpr/ppermute | solution.py:18
  198.0 5.3 %collective-permute-start.3 = (bf16[2,32,512]{1,2,0:T(8,128)(2,1)S(1)}, bf16[2,32,512]{1,2,0:T(8,128)(2,1)S(1)}, u32[]{:S(2)}, u32[]{:S(2)}) collective-permute-start(bf16[2,32,512]{1,2,0:T(8,128)(2,1)S(1)} %fusion.65), channel_id=1, source_target_pairs={{0,1},{1,2},{2,3},{3,4},{4,5},{5,6},{6,7},{7,8},{8,9},{9,10},{10,1... | collective-permute-start | bytes 196616 | tf_op jit(solution)/shard_map/while/body/eval_jaxpr/ppermute | solution.py:15
  205.6 10.6 %collective-permute-start.2 = (bf16[2,32,512]{1,2,0:T(8,128)(2,1)S(1)}, bf16[2,32,512]{1,2,0:T(8,128)(2,1)S(1)}, u32[]{:S(2)}, u32[]{:S(2)}) collective-permute-start(bf16[2,32,512]{1,2,0:T(8,128)(2,1)S(1)} %fusion.64), channel_id=1, source_target_pairs={{1,0},{2,1},{3,2},{4,3},{5,4},{6,5},{7,6},{8,7},{9,8},{10,9},{11,1... | collective-permute-start | bytes 196616 | tf_op jit(solution)/shard_map/while/body/eval_jaxpr/ppermute | solution.py:18
  214.2 5.3 %collective-permute-start.3 = (bf16[2,32,512]{1,2,0:T(8,128)(2,1)S(1)}, bf16[2,32,512]{1,2,0:T(8,128)(2,1)S(1)}, u32[]{:S(2)}, u32[]{:S(2)}) collective-permute-start(bf16[2,32,512]{1,2,0:T(8,128)(2,1)S(1)} %fusion.65), channel_id=1, source_target_pairs={{0,1},{1,2},{2,3},{3,4},{4,5},{5,6},{6,7},{7,8},{8,9},{9,10},{10,1... | collective-permute-start | bytes 196616 | tf_op jit(solution)/shard_map/while/body/eval_jaxpr/ppermute | solution.py:15
  221.9 10.6 %collective-permute-start.2 = (bf16[2,32,512]{1,2,0:T(8,128)(2,1)S(1)}, bf16[2,32,512]{1,2,0:T(8,128)(2,1)S(1)}, u32[]{:S(2)}, u32[]{:S(2)}) collective-permute-start(bf16[2,32,512]{1,2,0:T(8,128)(2,1)S(1)} %fusion.64), channel_id=1, source_target_pairs={{1,0},{2,1},{3,2},{4,3},{5,4},{6,5},{7,6},{8,7},{9,8},{10,9},{11,1... | collective-permute-start | bytes 196616 | tf_op jit(solution)/shard_map/while/body/eval_jaxpr/ppermute | solution.py:18
  230.6 5.3 %collective-permute-start.3 = (bf16[2,32,512]{1,2,0:T(8,128)(2,1)S(1)}, bf16[2,32,512]{1,2,0:T(8,128)(2,1)S(1)}, u32[]{:S(2)}, u32[]{:S(2)}) collective-permute-start(bf16[2,32,512]{1,2,0:T(8,128)(2,1)S(1)} %fusion.65), channel_id=1, source_target_pairs={{0,1},{1,2},{2,3},{3,4},{4,5},{5,6},{6,7},{7,8},{8,9},{9,10},{10,1... | collective-permute-start | bytes 196616 | tf_op jit(solution)/shard_map/while/body/eval_jaxpr/ppermute | solution.py:15
  238.2 10.6 %collective-permute-start.2 = (bf16[2,32,512]{1,2,0:T(8,128)(2,1)S(1)}, bf16[2,32,512]{1,2,0:T(8,128)(2,1)S(1)}, u32[]{:S(2)}, u32[]{:S(2)}) collective-permute-start(bf16[2,32,512]{1,2,0:T(8,128)(2,1)S(1)} %fusion.64), channel_id=1, source_target_pairs={{1,0},{2,1},{3,2},{4,3},{5,4},{6,5},{7,6},{8,7},{9,8},{10,9},{11,1... | collective-permute-start | bytes 196616 | tf_op jit(solution)/shard_map/while/body/eval_jaxpr/ppermute | solution.py:18
  246.8 5.3 %collective-permute-start.3 = (bf16[2,32,512]{1,2,0:T(8,128)(2,1)S(1)}, bf16[2,32,512]{1,2,0:T(8,128)(2,1)S(1)}, u32[]{:S(2)}, u32[]{:S(2)}) collective-permute-start(bf16[2,32,512]{1,2,0:T(8,128)(2,1)S(1)} %fusion.65), channel_id=1, source_target_pairs={{0,1},{1,2},{2,3},{3,4},{4,5},{5,6},{6,7},{7,8},{8,9},{9,10},{10,1... | collective-permute-start | bytes 196616 | tf_op jit(solution)/shard_map/while/body/eval_jaxpr/ppermute | solution.py:15
  254.5 10.6 %collective-permute-start.2 = (bf16[2,32,512]{1,2,0:T(8,128)(2,1)S(1)}, bf16[2,32,512]{1,2,0:T(8,128)(2,1)S(1)}, u32[]{:S(2)}, u32[]{:S(2)}) collective-permute-start(bf16[2,32,512]{1,2,0:T(8,128)(2,1)S(1)} %fusion.64), channel_id=1, source_target_pairs={{1,0},{2,1},{3,2},{4,3},{5,4},{6,5},{7,6},{8,7},{9,8},{10,9},{11,1... | collective-permute-start | bytes 196616 | tf_op jit(solution)/shard_map/while/body/eval_jaxpr/ppermute | solution.py:18
  263.1 5.3 %collective-permute-start.3 = (bf16[2,32,512]{1,2,0:T(8,128)(2,1)S(1)}, bf16[2,32,512]{1,2,0:T(8,128)(2,1)S(1)}, u32[]{:S(2)}, u32[]{:S(2)}) collective-permute-start(bf16[2,32,512]{1,2,0:T(8,128)(2,1)S(1)} %fusion.65), channel_id=1, source_target_pairs={{0,1},{1,2},{2,3},{3,4},{4,5},{5,6},{6,7},{7,8},{8,9},{9,10},{10,1... | collective-permute-start | bytes 196616 | tf_op jit(solution)/shard_map/while/body/eval_jaxpr/ppermute | solution.py:15
  270.8 10.6 %collective-permute-start.2 = (bf16[2,32,512]{1,2,0:T(8,128)(2,1)S(1)}, bf16[2,32,512]{1,2,0:T(8,128)(2,1)S(1)}, u32[]{:S(2)}, u32[]{:S(2)}) collective-permute-start(bf16[2,32,512]{1,2,0:T(8,128)(2,1)S(1)} %fusion.64), channel_id=1, source_target_pairs={{1,0},{2,1},{3,2},{4,3},{5,4},{6,5},{7,6},{8,7},{9,8},{10,9},{11,1... | collective-permute-start | bytes 196616 | tf_op jit(solution)/shard_map/while/body/eval_jaxpr/ppermute | solution.py:18
  279.4 5.3 %collective-permute-start.3 = (bf16[2,32,512]{1,2,0:T(8,128)(2,1)S(1)}, bf16[2,32,512]{1,2,0:T(8,128)(2,1)S(1)}, u32[]{:S(2)}, u32[]{:S(2)}) collective-permute-start(bf16[2,32,512]{1,2,0:T(8,128)(2,1)S(1)} %fusion.65), channel_id=1, source_target_pairs={{0,1},{1,2},{2,3},{3,4},{4,5},{5,6},{6,7},{7,8},{8,9},{9,10},{10,1... | collective-permute-start | bytes 196616 | tf_op jit(solution)/shard_map/while/body/eval_jaxpr/ppermute | solution.py:15
Sparse Core Ops, SparseCore 0:
  287.3 86.6 all-gather.2
